TPU v7x, 1024 devices: a whole 8x8x8 slice. The times are simulated.
1024 devices in a mesh: row: 64 (over y, x), col: 16 (over z, core).
Axes of the slice: x: 8, y: 8, z: 8, core: 2. Of those that a mesh axis runs over, the one named last changes fastest.
Arguments:
- density: bfloat16 [4096, 4096], P('row', 'col'), may hold values from -1 to 1, as said below
- branches: int32 [4], replicated, may hold values from 0 to 1, as said below
- keep: int32 [4, 32, 32], replicated, may hold values from 0 to 1, as said below
Outputs:
- purified: bfloat16 [4096, 4096], P('row', 'col')
- traces: float32 [4, 2], replicated
- occupations: float32 [4096], P('row')
Inputs may be any that keep to these rules, and one draw needn't show every extreme that they name: density is exactly symmetric. `branches`: exactly half of the 4 steps take the square. Each keep[s] is symmetric in its two block indices and holds 1 on every diagonal block.
All inputs are finite; a program needn't handle non-finite values.
Results may differ from a plain program's by a relative error of at most 0.0077.
Values may be sent and summed in bfloat16 or wider, within the bound.
A program may use at most 32 MiB of HBM per device.

v0:
```python
import jax
import jax.numpy as jnp
from jax import lax
from jax.sharding import PartitionSpec as P

B = 128
NB = 32
STEPS = 4


def block_weights(keep_section, row_offset, col_offset, tile_rows, tile_cols):
    count = keep_section.shape[0]
    row_blocks = (row_offset + jnp.arange(tile_rows)) // B
    col_blocks = (col_offset + jnp.arange(tile_cols)) // B
    choose_rows = (row_blocks[:, None] == jnp.arange(count)[None, :]).astype(jnp.float32)
    choose_cols = (col_blocks[:, None] == jnp.arange(count)[None, :]).astype(jnp.float32)
    spread_rows = jnp.dot(choose_rows, keep_section.astype(jnp.float32))
    return jnp.dot(spread_rows, choose_cols.T)


def body(density, branches, keep):
    tile_rows, tile_cols = density.shape
    order = NB * B
    row_offset = lax.axis_index("row") * tile_rows
    col_offset = lax.axis_index("col") * tile_cols
    global_rows = row_offset + jnp.arange(tile_rows)
    global_cols = col_offset + jnp.arange(tile_cols)
    diagonal_mask = global_rows[:, None] == global_cols[None, :]
    on_diagonal = diagonal_mask.astype(jnp.float32)
    current = density
    collected = []
    occupations = jnp.zeros((tile_rows,), jnp.float32)
    for section in range(STEPS):
        local_one = jnp.sum(current.astype(jnp.float32) * on_diagonal)
        whole_rows = lax.all_gather(current, "col", axis=1, tiled=True)
        square = jnp.dot(
            whole_rows,
            lax.all_gather(current, "row", axis=0, tiled=True),
            preferred_element_type=jnp.float32,
        )
        local_two = jnp.sum(square * on_diagonal)
        local_pair = jnp.stack([local_one, local_two])
        collected.append(lax.psum(local_pair, ("row", "col")))
        if section == STEPS - 1:
            diag_square = jnp.einsum(
                "ik,ik->i", whole_rows, whole_rows, preferred_element_type=jnp.float32
            )
            own_columns = jnp.arange(whole_rows.shape[1])[None, :] == global_rows[:, None]
            diag_current = jnp.sum(
                jnp.where(own_columns, whole_rows, jnp.zeros_like(whole_rows)).astype(jnp.float32),
                axis=1,
            )
            occupations = jnp.where(
                branches[section] == 1, diag_square, 2.0 * diag_current - diag_square
            )
        weights = block_weights(keep[section], row_offset, col_offset, tile_rows, tile_cols)
        grown = jnp.where(
            branches[section] == 1, square, 2.0 * current.astype(jnp.float32) - square
        )
        current = (grown * weights).astype(jnp.bfloat16)
    stacked = jnp.stack(collected)
    purified = jnp.where(diagonal_mask, jnp.zeros_like(current), current)
    return (purified, stacked / order, occupations)


def solution(mesh):
    return jax.shard_map(
        body,
        mesh=mesh,
        in_specs=(P("row", "col"), P(), P()),
        out_specs=(P("row", "col"), P(), P("row")),
        check_vma=False,
    )
```

profile of v0, /device:TPU:1, one launch (start us, length us, event | category | flops | bytes accessed | tf_op | source)
XLA Modules:
  0.0 516.4 jit_solution(12550189597367995631)
XLA Ops:
  7.2 0.0 copy-start
  7.2 0.0 all-gather.5.cloned.1.call-start
  7.2 0.7 all-gather.5.cloned.1.call-update
  7.9 0.0 all-gather.7.cloned.1.call-start
  8.0 1.4 fusion.59
  10.1 32.5 %all_gather.24 = bf16[64,4096]{1,0:T(8,128)(2,1)S(1)} all-gather(bf16[64,256]{1,0:T(8,128)(2,1)} %param.3), channel_id=1, replica_groups=mesh['row'=64,'col'=16] {'col'}, dimensions={1}, use_global_device_ids=true | all-gather | bytes 557056 | tf_op jit(solution)/shard_map/all_gather | solution.py:35
  42.6 66.2 %all-gather.5.cloned.1.call-done = bf16[4096,256]{1,0:T(8,128)(2,1)} async-done(((bf16[64,256]{1,0:T(8,128)(2,1)}), bf16[4096,256]{1,0:T(8,128)(2,1)}) %all-gather.5.cloned.1.call-update) | async-done | bytes 2097168 | tf_op jit(solution)/shard_map/all_gather | solution.py:38
  108.8 2.0 fusion.60
  110.9 0.9 fusion
  111.8 0.0 all-gather.7.cloned.1.call-update
  111.9 0.0 all-gather.9.cloned.1.call-start
  112.5 25.6 %all_gather.26 = bf16[64,4096]{1,0:T(8,128)(2,1)S(1)} all-gather(bf16[64,256]{1,0:T(8,128)(2,1)} %fusion), channel_id=1, replica_groups=mesh['row'=64,'col'=16] {'col'}, dimensions={1}, use_global_device_ids=true | all-gather | bytes 557056 | tf_op jit(solution)/shard_map/all_gather | solution.py:35
  138.1 62.4 %all-gather.7.cloned.1.call-done = bf16[4096,256]{1,0:T(8,128)(2,1)} async-done(((bf16[64,256]{1,0:T(8,128)(2,1)}), bf16[4096,256]{1,0:T(8,128)(2,1)}) %all-gather.7.cloned.1.call-update) | async-done | bytes 2097168 | tf_op jit(solution)/shard_map/all_gather | solution.py:38
  200.5 2.0 fusion.61
  202.6 0.9 fusion.1
  203.5 0.0 all-gather.9.cloned.1.call-update
  203.6 0.0 all-gather.11.cloned.1.call-start
  204.2 25.6 %all_gather.28 = bf16[64,4096]{1,0:T(8,128)(2,1)S(1)} all-gather(bf16[64,256]{1,0:T(8,128)(2,1)} %fusion.1), channel_id=1, replica_groups=mesh['row'=64,'col'=16] {'col'}, dimensions={1}, use_global_device_ids=true | all-gather | bytes 557056 | tf_op jit(solution)/shard_map/all_gather | solution.py:35
  229.9 62.4 %all-gather.9.cloned.1.call-done = bf16[4096,256]{1,0:T(8,128)(2,1)} async-done(((bf16[64,256]{1,0:T(8,128)(2,1)}), bf16[4096,256]{1,0:T(8,128)(2,1)}) %all-gather.9.cloned.1.call-update) | async-done | bytes 2097168 | tf_op jit(solution)/shard_map/all_gather | solution.py:38
  292.2 2.0 fusion.62
  294.3 0.9 fusion.2
  295.2 0.0 all-gather.11.cloned.1.call-update
  295.9 25.6 %all_gather.30 = bf16[64,4096]{1,0:T(8,128)(2,1)S(1)} all-gather(bf16[64,256]{1,0:T(8,128)(2,1)} %fusion.2), channel_id=1, replica_groups=mesh['row'=64,'col'=16] {'col'}, dimensions={1}, use_global_device_ids=true | all-gather | bytes 557056 | tf_op jit(solution)/shard_map/all_gather | solution.py:35
  321.5 0.4 convert_reduce_fusion
  321.9 0.5 broadcast_select_fusion
  322.4 61.4 %all-gather.11.cloned.1.call-done = bf16[4096,256]{1,0:T(8,128)(2,1)} async-done(((bf16[64,256]{1,0:T(8,128)(2,1)}), bf16[4096,256]{1,0:T(8,128)(2,1)}) %all-gather.11.cloned.1.call-update) | async-done | bytes 2097168 | tf_op jit(solution)/shard_map/all_gather | solution.py:38
  383.8 2.7 fusion.15
  386.5 0.9 fusion.4
  387.5 2.6 maximum_bitcast_fusion
  390.0 2.4 maximum_bitcast_fusion.2
  392.4 116.8 %all-reduce = (f32[1,2]{1,0:T(1,128)S(1)}, f32[1,2]{1,0:T(1,128)S(1)}, f32[1,2]{1,0:T(1,128)S(1)}, f32[1,2]{1,0:T(1,128)S(1)}) all-reduce(f32[1,2]{1,0:T(1,128)S(1)} %get-tuple-element.28, f32[1,2]{1,0:T(1,128)S(1)} %get-tuple-element.27, f32[1,2]{1,0:T(1,128)S(1)} %get-tuple-element.26, ...), channel_id=1, replica_groups=mesh['row'=64,'col'=16] {'row','col'}, use_global_device_ids=true, to_apply=%region_11.12 | all-reduce | flops 8 | bytes 64 | tf_op jit(solution)/shard_map/psum | solution.py:43
  509.2 0.7 copy.6
  (14 shorter events, 0.1 us)
Async XLA Ops:
  7.2 103.7 %copy-start = (bf16[64,256]{1,0:T(8,128)(2,1)S(1)}, bf16[64,256]{1,0:T(8,128)(2,1)}, u32[]{:S(2)}) copy-start(bf16[64,256]{1,0:T(8,128)(2,1)} %param.3) | copy-start | bytes 98308
  7.2 103.7 %copy-start.4 = (s32[4,32,32]{2,1,0:T(8,128)S(1)}, s32[4,32,32]{2,1,0:T(8,128)}, u32[]{:S(2)}) copy-start(s32[4,32,32]{2,1,0:T(8,128)} %param.5) | copy-start | bytes 49156
  7.2 101.6 %all-gather.5.cloned.1.call-start = ((), (), s32[]{:S(2)}) async-start(), calls=%async_computation | async-start | bytes 2129920 | tf_op jit(solution)/shard_map/all_gather | solution.py:38
  7.9 192.6 %all-gather.7.cloned.1.call-start = ((), (), s32[]{:S(2)}) async-start(), calls=%async_computation.1 | async-start | bytes 2129920 | tf_op jit(solution)/shard_map/all_gather | solution.py:38
  111.8 90.7 %copy-start.1 = (bf16[64,256]{1,0:T(8,128)(2,1)S(1)}, bf16[64,256]{1,0:T(8,128)(2,1)}, u32[]{:S(2)}) copy-start(bf16[64,256]{1,0:T(8,128)(2,1)} %fusion) | copy-start | bytes 98308
  111.9 180.4 %all-gather.9.cloned.1.call-start = ((), (), s32[]{:S(2)}) async-start(), calls=%async_computation.2 | async-start | bytes 2129920 | tf_op jit(solution)/shard_map/all_gather | solution.py:38
  203.5 90.8 %copy-start.2 = (bf16[64,256]{1,0:T(8,128)(2,1)S(1)}, bf16[64,256]{1,0:T(8,128)(2,1)}, u32[]{:S(2)}) copy-start(bf16[64,256]{1,0:T(8,128)(2,1)} %fusion.1) | copy-start | bytes 98308
  203.6 180.2 %all-gather.11.cloned.1.call-start = ((), (), s32[]{:S(2)}) async-start(), calls=%async_computation.3 | async-start | bytes 2129920 | tf_op jit(solution)/shard_map/all_gather | solution.py:38
  295.2 91.3 %copy-start.3 = (bf16[64,256]{1,0:T(8,128)(2,1)S(1)}, bf16[64,256]{1,0:T(8,128)(2,1)}, u32[]{:S(2)}) copy-start(bf16[64,256]{1,0:T(8,128)(2,1)} %fusion.2) | copy-start | bytes 98308
Sparse Core Ops, SparseCore 0:
  12.3 96.5 all-gather.4
  113.6 86.8 all-gather.6
  205.3 86.8 all-gather.8
  296.9 86.8 all-gather.10
where the time goes:
time: 517 us; the launch traced here: 516 us
  waiting for transfers between devices  253 us (49%)
  blocking collectives  226 us (44%)
  between operations  16.4 us (3%)
  matrix products  12.6 us (2%)
  other arithmetic  5.9 us (1%)
    all_gather x4, waiting for transfers between devices, body(): lax.all_gather(current, 'row', axis=0, tiled=True)  252 us
    psum x1, blocking collectives, body(): collected.append(lax.psum(local_pair, ('row', 'col')))  117 us
    all_gather x4, blocking collectives, body(): whole_rows = lax.all_gather(current, 'col', axis=1, tiled=True)  109 us
  transfers between devices with their start and end apart: 4, of which 4 were waited for; matrix products, arithmetic and copies ran while one was open for 0% of the time, Pallas kernels for 0%

commit v1 on v0

v1 whole, which is shorter than its diff:
```python
import functools

import jax
import jax.numpy as jnp
from jax import lax
from jax.experimental import pallas as pl
from jax.experimental.pallas import tpu as pltpu
from jax.sharding import PartitionSpec as P

B = 128
LANES = 128
STEPS = 4
H = 2
MESH = pl.DeviceIdType.MESH
F32 = jnp.float32
BF16 = jnp.bfloat16
NT = (((1,), (1,)), ((), ()))


def kernel(G, bs, dens, branches_in, keep_in, out, traces, occ,
           a2, a3, p1, n1, h1, d1, cur, es, rr, vz, vs, vy, branches, keep,
           in_s, ax_s, ax_r, au_s, au_r, rs_s, rs_r, dd_s, dd_r, es_s, es_r, vs_s, vs_r, sb_s, sb_r):
    half, slab = bs // 2, bs // G
    order = G * bs
    row, col = lax.axis_index("row"), lax.axis_index("col")
    x, y, z, c = lax.rem(row, G), row // G, col // 2, lax.rem(col, 2)
    xs = pl.multiple_of(x * slab, slab)
    mine = pl.multiple_of(c * half, half)
    theirs = pl.multiple_of((1 - c) * half, half)

    def dev(ax, ay, az, ac):
        return {"row": ay * G + ax, "col": az * 2 + ac}

    far_first = sorted(range(1, G), key=lambda d: -min(d, G - d))
    pos = {"x": {d: lax.rem(x + d, G) for d in far_first},
           "y": {d: lax.rem(y + d, G) for d in far_first},
           "z": {d: lax.rem(z + d, G) for d in far_first}}
    ids = {"x": {d: dev(pos["x"][d], y, z, c) for d in far_first},
           "y": {d: dev(x, pos["y"][d], z, c) for d in far_first},
           "z": {d: dev(x, y, pos["z"][d], c) for d in far_first}}
    here = {"x": x, "y": y, "z": z}
    sib = dev(x, y, z, 1 - c)

    def copy(src, dst, ssem, rsem, target):
        return pltpu.make_async_remote_copy(
            src_ref=src, dst_ref=dst, send_sem=ssem, recv_sem=rsem,
            device_id=target, device_id_type=MESH)

    def got(ref, sem):
        copy(ref, ref, sem, sem, sib).wait_recv()

    def left(ref, sem):
        copy(ref, ref, sem, sem, sib).wait_send()

    fetch = [pltpu.make_async_copy(dens, a2.at[0, pl.ds(xs, slab)], in_s.at[0]),
             pltpu.make_async_copy(dens, a3.at[0, pl.ds(pl.multiple_of(y * slab, slab), slab)], in_s.at[1]),
             pltpu.make_async_copy(keep_in, keep, in_s.at[2]),
             pltpu.make_async_copy(branches_in, branches, in_s.at[3])]
    for cp in fetch:
        cp.start()
    barrier = pltpu.get_barrier_semaphore()
    for d in far_first:
        for axis in ("x", "y", "z"):
            pl.semaphore_signal(barrier, inc=1, device_id=ids[axis][d], device_id_type=MESH)
    pl.semaphore_signal(barrier, inc=1, device_id=sib, device_id_type=MESH)
    fetch[0].wait()
    fetch[1].wait()
    pl.semaphore_wait(barrier, 3 * (G - 1) + 1)

    sub = slab // H
    line = a2.at[0, pl.ds(0, (G - 1) * slab)]

    def gather(p, axis, h):
        two = a2.at[p, pl.ds(pl.multiple_of(xs + h * sub, sub), sub)]
        three = a3.at[p, pl.ds(pl.multiple_of(here[axis] * slab + h * sub, sub), sub)]
        for d in far_first:
            copy(two, two, ax_s, ax_r.at[p], ids["x"][d]).start()
            copy(three, three, au_s, au_r.at[p], ids[axis][d]).start()

    iota = functools.partial(lax.broadcasted_iota, jnp.int32)
    pick = jnp.where(iota((slab, half), 1) == x * slab - c * half + iota((slab, half), 0), 0.5, 0.0).astype(BF16)
    row_here = (x * slab) // half == c
    on_block = jnp.where(y == z, 1.0, 0.0).astype(F32)
    block_diag = jnp.where(iota((half, half), 0) == iota((half, half), 1), on_block, 0.0)

    t_one, t_two = [], []

    for h in range(H):
        gather(0, "y", h)
    fetch[2].wait()
    fetch[3].wait()

    for s in range(STEPS):
        p = s % 2
        n = 1 - p
        last = s == STEPS - 1
        au, av = ("y", "z") if p == 0 else ("z", "y")
        u, v = here[au], here[av]
        us = pl.multiple_of(u * slab, slab)
        vs_at = pl.multiple_of(v * slab, slab)

        got(line, ax_r.at[p])
        got(line, au_r.at[p])
        far = a2[p, pl.ds(theirs, half), :]
        near = a2[p, pl.ds(mine, half), :]
        h1[p] = lax.dot_general(a3[p], far, NT, preferred_element_type=F32).astype(BF16)

        @pl.when(row_here)
        def _():
            e = lax.dot_general(pick, far, NT, preferred_element_type=F32)
            own = lax.dot_general(a3[p, pl.ds(vs_at, slab), :], far, NT, preferred_element_type=F32)
            h1[p, pl.ds(vs_at, slab), :] = (own - e).astype(BF16)
            es[p] = (2.0 * e).astype(BF16)
            copy(es.at[p], cur.at[p], es_s.at[p], es_r.at[p], sib).start()

        copy(h1.at[p], d1.at[p], dd_s.at[p], dd_r.at[p], sib).start()
        n1[...] = lax.dot_general(a3[p], near, NT, preferred_element_type=F32) - (0.5 * on_block) * a3[p].astype(F32)

        @pl.when(row_here)
        def _():
            e = lax.dot_general(pick, near, NT, preferred_element_type=F32)
            n1[pl.ds(vs_at, slab), :] = n1[pl.ds(vs_at, slab), :] - e
            cur[p] = (2.0 * e).astype(BF16)

        got(d1.at[p], dd_r.at[p])
        p1[p] = (n1[...] + d1[p].astype(F32)).astype(BF16)
        if s > 0:
            left(line, rs_s)
        for h in range(H):
            for d in far_first:
                copy(p1.at[p, pl.ds(pl.multiple_of(pos[av][d] * slab + h * sub, sub), sub)],
                     rr.at[p, h, v], rs_s, rs_r.at[p, h], ids[av][d]).start()
        for h in range(H):
            rr[p, h, v] = p1[p, pl.ds(pl.multiple_of(v * slab + h * sub, sub), sub), :]

        whole = a2[p].astype(F32)
        squares = jnp.sum(whole * whole, axis=0, keepdims=True)
        diagonal = jnp.sum(a2[p, pl.ds(mine, half), :].astype(F32) * block_diag, axis=0, keepdims=True)
        t_one.append(jnp.sum(diagonal, axis=1, keepdims=True))
        t_two.append(jnp.sum(squares, axis=1, keepdims=True))

        left(line, ax_s)
        left(line, au_s)
        left(h1.at[p], dd_s.at[p])

        @pl.when(row_here)
        def _():
            left(es.at[p], es_s.at[p])

        @pl.when(jnp.logical_not(row_here))
        def _():
            got(cur.at[p], es_r.at[p])

        if last:
            lane, deep = iota((1, half), 1), iota((8, half), 0)
            trow = jnp.zeros((1, half), F32)
            for i in range(STEPS):
                trow = trow + jnp.where(lane == 2 * i, t_one[i], 0.0) + jnp.where(lane == 2 * i + 1, t_two[i], 0.0)
            vz[z] = (jnp.where(deep == 0, squares, 0.0) + jnp.where(deep == 1, diagonal, 0.0)
                     + jnp.where(deep == 2, trow, 0.0))
            for d in far_first:
                copy(vz.at[z], vz.at[z], vs_s.at[0], vs_r.at[0], ids["z"][d]).start()
            got(vz.at[pl.ds(0, G - 1)], vs_r.at[0])
            vs[c] = jnp.sum(vz[...], axis=0)
            copy(vs.at[c], vs.at[c], sb_s, sb_r, sib).start()
            got(vs.at[0], sb_r)
            vy[y] = (vs[0] + vs[1])[:, :LANES]
            for d in far_first:
                copy(vy.at[y], vy.at[y], vs_s.at[1], vs_r.at[1], ids["y"][d]).start()
            mid = jnp.where(x * slab < half, vs[0], vs[1])
            f = branches[s].astype(F32)
            grown = f * mid[0:1, :] + (1.0 - f) * (2.0 * mid[1:2, :] - mid[0:1, :])
            shown = iota((slab, half), 1) == lax.rem(x * slab, half) + iota((slab, half), 0)
            column = jnp.sum(jnp.where(shown, grown, 0.0), axis=1, keepdims=True)
            eye = iota((slab, slab), 0) == iota((slab, slab), 1)
            occ[...] = jnp.sum(jnp.where(eye, column, 0.0), axis=0, keepdims=True)

        f = branches[s].astype(F32)
        fa, fb = 2.0 * f - 1.0, 2.0 - 2.0 * f
        for h in range(H):
            rs = slice(h * sub, (h + 1) * sub)
            rb = (v * bs + x * slab + h * sub) // B
            cb = (u * bs + c * half) // B
            at2 = pl.multiple_of(xs + h * sub, sub)
            at3 = pl.multiple_of(v * slab + h * sub, sub)
            got(rr.at[p, h, pl.ds(0, G - 1)], rs_r.at[p, h])
            now = cur[p, rs, :].astype(F32)
            grown = fa * (jnp.sum(rr[p, h].astype(F32), axis=0) + now) + fb * now
            if last:
                grown = jnp.where(v * bs + x * slab + h * sub + iota((sub, half), 0)
                                  == u * bs + c * half + iota((sub, half), 1), 0.0, grown)
            for q in range(half // B):
                cs = slice(q * B, (q + 1) * B)
                new = (grown[:, cs] * keep[s, rb, cb + q].astype(F32)).astype(BF16)
                if last:
                    out[rs, cs] = new
                else:
                    a2[n, pl.ds(at2, sub), cs] = new
                    a3[n, pl.ds(at3, sub), cs] = new
            if not last:
                gather(n, av, h)

    got(vy.at[pl.ds(0, G - 1)], vs_r.at[1])
    tr = jnp.sum(vy[...], axis=0)[2:3, :] * (1.0 / order)
    lane, deep = iota((STEPS, LANES), 1), iota((STEPS, LANES), 0)
    for k in range(2):
        traces[:, k:k + 1] = jnp.sum(jnp.where(lane == 2 * deep + k, tr, 0.0), axis=1, keepdims=True)
    left(line, rs_s)
    left(vz.at[pl.ds(0, G - 1)], vs_s.at[0])
    left(vy.at[pl.ds(0, G - 1)], vs_s.at[1])
    left(vs.at[0], sb_s)


def body(G, density, branches, keep):
    slab, half = density.shape
    bs = 2 * half
    v, dma = pltpu.VMEM, pltpu.SemaphoreType.DMA
    vmem, hbm = pl.BlockSpec(memory_space=pltpu.VMEM), pl.BlockSpec(memory_space=pltpu.HBM)
    purified, traces, occ = pl.pallas_call(
        functools.partial(kernel, G, bs),
        out_shape=(jax.ShapeDtypeStruct((slab, half), BF16),
                   jax.ShapeDtypeStruct((STEPS, 2), F32),
                   jax.ShapeDtypeStruct((1, slab), F32)),
        in_specs=[hbm, hbm, hbm],
        out_specs=(vmem, vmem, vmem),
        scratch_shapes=[
            v((2, bs, half), BF16), v((2, bs, half), BF16), v((2, bs, half), BF16), v((bs, half), F32),
            v((2, bs, half), BF16), v((2, bs, half), BF16), v((2, slab, half), BF16), v((2, slab, half), BF16),
            v((2, H, G, slab // H, half), BF16),
            v((G, 8, half), F32), v((2, 8, half), F32), v((G, 8, LANES), F32),
            pltpu.SMEM(branches.shape, jnp.int32), pltpu.SMEM(keep.shape, jnp.int32),
            dma((4,)), dma, dma((2,)), dma, dma((2,)), dma, dma((2, H)), dma((2,)), dma((2,)),
            dma((2,)), dma((2,)), dma((2,)), dma((2,)), dma, dma,
        ],
        compiler_params=pltpu.CompilerParams(
            collective_id=0, has_side_effects=True, vmem_limit_bytes=60 * 1024 * 1024),
        name="purify",
    )(density, branches, keep)
    return purified, traces, occ.reshape(slab)


def solution(mesh):
    G = mesh.shape["col"] // 2
    return jax.shard_map(
        functools.partial(body, G),
        mesh=mesh,
        in_specs=(P("row", "col"), P(), P()),
        out_specs=(P("row", "col"), P(), P("row")),
        check_vma=False,
    )
```

time: 517 us -> 95.9 us (0.19)
  waiting for transfers between devices: 253 us -> 0 us
  blocking collectives: 226 us -> 0 us
  Pallas kernels: 0 us -> 91.7 us
  between operations: 16.4 us -> 0.65 us
  matrix products: 12.6 us -> 0 us
  other arithmetic: 5.9 us -> 0 us
    all_gather x4 -> x0, waiting for transfers between devices: 252 us -> none  [body(): lax.all_gather(current, 'row', axis=0, tiled=True)]
    psum x1 -> x0, blocking collectives: 117 us -> none  [body(): collected.append(lax.psum(local_pair, ('row', 'col')))]
    all_gather x4 -> x0, blocking collectives: 109 us -> none  [body(): whole_rows = lax.all_gather(current, 'col', axis=1, tiled=True)]
    pallas_call x0 -> x1, Pallas kernels: none -> 91.7 us  [body(): pl.pallas_call(functools.partial(kernel, G, bs), out_shape=(jax.ShapeDtyp...]
    dot_general x8 -> x0, matrix products: 12.6 us -> none  [the longest x4 8.87 us: body(): jnp.dot(whole_rows, lax.all_gather(current, 'row', axis=0, tiled=True), p...]
  transfers between devices with their start and end apart: 4 -> 0, of which waited for: 4 -> 0; matrix products, arithmetic and copies ran while one was open for 0% -> 0% of each run, Pallas kernels for 0% -> 0%
where the time goes in v1:
time: 95.9 us; the launch traced here: 95.6 us
  Pallas kernels  91.7 us (96%)
  local copies, waits for them, and re-layouts  3.2 us (3%)
    pallas_call x1, Pallas kernels, body(): pl.pallas_call(functools.partial(kernel, G, bs), out_shape=(jax.ShapeDtyp...  91.7 us
    unnamed x7, local copies, waits for them, and re-layouts  3.2 us

profile of v1, /device:TPU:1, one launch (start us, length us, event | category | flops | bytes accessed | tf_op | source)
XLA Modules:
  0.0 95.6 jit_solution(121999030969906865)
XLA Ops:
  0.6 91.7 %purify.1 = (bf16[64,256]{1,0:T(8,128)(2,1)}, f32[4,2]{1,0:T(4,128)}, f32[1,64]{1,0:T(1,128)}) custom-call(bf16[64,256]{1,0:T(8,128)(2,1)} %dens.1, s32[4]{0:T(128)} %branches_in.1, s32[4,32,32]{2,1,0:T(8,128)} %keep_in.1), custom_call_target="tpu_custom_call" | custom-call | tf_op jit(solution)/shard_map/purify/pallas_call | solution.py:219
  92.4 0.0 copy-start
  92.4 0.7 copy-done
  93.1 0.6 copy.6
  93.7 0.0 copy-start.1
  93.7 1.4 %copy.9 = bf16[64,256]{1,0:T(8,128)(2,1)} copy(bf16[64,256]{1,0:T(8,128)(2,1)} %get-tuple-element.15) | data formatting | bytes 65536
  95.1 0.0 copy-done.1
  95.1 0.5 copy.10
Async XLA Ops:
  92.4 0.7 copy-start
  93.7 1.4 %copy-start.1 = (f32[1,64]{1,0:T(1,128)S(1)}, f32[1,64]{1,0:T(1,128)}, u32[]{:S(2)}) copy-start(f32[1,64]{1,0:T(1,128)} %get-tuple-element.8) | copy-start | bytes 772

commit v2 on v1

v2 whole, which is shorter than its diff:
```python
import functools

import jax
import jax.numpy as jnp
from jax import lax
from jax.experimental import pallas as pl
from jax.experimental.pallas import tpu as pltpu
from jax.sharding import PartitionSpec as P

B = 128
LANES = 128
STEPS = 4
H = 2
MESH = pl.DeviceIdType.MESH
F32 = jnp.float32
BF16 = jnp.bfloat16
NT = (((1,), (1,)), ((), ()))


def kernel(G, bs, dens, branches_in, keep_in, out, traces, occ,
           a2, a3, p1, n1, h1, d1, cur, es, ed, rr, vx, vz, vs, vy, branches, keep,
           in_s, ax_s, ax_r, au_s, au_r, rs_s, rs_r, dd_s, dd_r, es_s, es_r, vs_s, vs_r, sb_s, sb_r):
    half, slab = bs // 2, bs // G
    order = G * bs
    row, col = lax.axis_index("row"), lax.axis_index("col")
    x, y, z, c = lax.rem(row, G), row // G, col // 2, lax.rem(col, 2)
    xs = pl.multiple_of(x * slab, slab)
    mine = pl.multiple_of(c * half, half)
    theirs = pl.multiple_of((1 - c) * half, half)

    def dev(ax, ay, az, ac):
        return {"row": ay * G + ax, "col": az * 2 + ac}

    far_first = sorted(range(1, G), key=lambda d: -min(d, G - d))
    pos = {"x": {d: lax.rem(x + d, G) for d in far_first},
           "y": {d: lax.rem(y + d, G) for d in far_first},
           "z": {d: lax.rem(z + d, G) for d in far_first}}
    ids = {"x": {d: dev(pos["x"][d], y, z, c) for d in far_first},
           "y": {d: dev(x, pos["y"][d], z, c) for d in far_first},
           "z": {d: dev(x, y, pos["z"][d], c) for d in far_first}}
    here = {"x": x, "y": y, "z": z}
    sib = dev(x, y, z, 1 - c)

    def copy(src, dst, ssem, rsem, target):
        return pltpu.make_async_remote_copy(
            src_ref=src, dst_ref=dst, send_sem=ssem, recv_sem=rsem,
            device_id=target, device_id_type=MESH)

    def got(ref, sem):
        copy(ref, ref, sem, sem, sib).wait_recv()

    def left(ref, sem):
        copy(ref, ref, sem, sem, sib).wait_send()

    part = half // H
    fetch = []
    for h in range(H):
        src = dens.at[:, pl.ds(h * part, part)]
        fetch.append(pltpu.make_async_copy(src, a2.at[0, h, pl.ds(xs, slab)], in_s.at[2 * h]))
        fetch.append(pltpu.make_async_copy(
            src, a3.at[0, h, pl.ds(pl.multiple_of(y * slab, slab), slab)], in_s.at[2 * h + 1]))
    fetch.append(pltpu.make_async_copy(keep_in, keep, in_s.at[2 * H]))
    fetch.append(pltpu.make_async_copy(branches_in, branches, in_s.at[2 * H + 1]))
    for cp in fetch:
        cp.start()
    barrier = pltpu.get_barrier_semaphore()
    for d in far_first:
        for axis in ("x", "y", "z"):
            pl.semaphore_signal(barrier, inc=1, device_id=ids[axis][d], device_id_type=MESH)
    pl.semaphore_signal(barrier, inc=1, device_id=sib, device_id_type=MESH)
    for cp in fetch[:2 * H]:
        cp.wait()
    pl.semaphore_wait(barrier, 3 * (G - 1) + 1)

    line = a2.at[0, :, pl.ds(0, (G - 1) * slab)]

    def gather(p, axis, h):
        two = a2.at[p, h, pl.ds(xs, slab)]
        three = a3.at[p, h, pl.ds(pl.multiple_of(here[axis] * slab, slab), slab)]
        for d in far_first:
            copy(three, three, au_s, au_r.at[p], ids[axis][d]).start()
        for d in far_first:
            copy(two, two, ax_s, ax_r.at[p], ids["x"][d]).start()

    iota = functools.partial(lax.broadcasted_iota, jnp.int32)
    pick = jnp.where(iota((slab, half), 1) == x * slab - c * half + iota((slab, half), 0), 0.5, 0.0).astype(BF16)
    row_here = (x * slab) // half == c
    on_block = jnp.where(y == z, 1.0, 0.0).astype(F32)
    own_diag = jnp.where(iota((slab, half), 0) + x * slab == iota((slab, half), 1) + c * half, on_block, 0.0)

    t_one, t_two = [], []

    def across(ref, p, start, size):
        return jnp.concatenate([ref[p, k, pl.ds(start, size), :] for k in range(H)], axis=1)

    def note_traces(p):
        shard = across(a2, p, xs, slab).astype(F32)
        squares = jnp.sum(shard * shard, axis=0, keepdims=True)
        diagonal = jnp.sum(shard * own_diag, axis=0, keepdims=True)
        t_one.append(jnp.sum(diagonal, axis=1, keepdims=True))
        t_two.append(jnp.sum(squares, axis=1, keepdims=True))
        return squares, diagonal

    for h in range(H):
        gather(0, "y", h)
    note_traces(0)
    fetch[2 * H].wait()
    fetch[2 * H + 1].wait()

    for s in range(STEPS):
        p = s % 2
        n = 1 - p
        last = s == STEPS - 1
        au, av = ("y", "z") if p == 0 else ("z", "y")
        u, v = here[au], here[av]
        us = pl.multiple_of(u * slab, slab)
        vs_at = pl.multiple_of(v * slab, slab)

        if last:
            got(vx.at[pl.ds(0, G - 1)], vs_r.at[1])
            vz[z] = jnp.sum(vx[...], axis=0)
            for d in far_first:
                copy(vz.at[z], vz.at[z], vs_s.at[0], vs_r.at[0], ids["z"][d]).start()
        got(line, ax_r.at[p])
        got(line, au_r.at[p])
        rows3 = across(a3, p, 0, bs)
        for h in range(H):
            h1[p, h] = lax.dot_general(rows3, across(a2, p, pl.multiple_of(theirs + h * part, part), part), NT,
                                       preferred_element_type=F32).astype(BF16)
            copy(h1.at[p, h], d1.at[p, h], dd_s.at[p], dd_r.at[p, h], sib).start()
        if s > 0:
            left(line, rs_s)
        for h in range(H):
            n1[h] = lax.dot_general(rows3, across(a2, p, pl.multiple_of(mine + h * part, part), part), NT,
                                    preferred_element_type=F32) - (0.5 * on_block) * a3[p, h].astype(F32)
            got(d1.at[p, h], dd_r.at[p, h])
            p1[p, h] = (n1[h] + d1[p, h].astype(F32)).astype(BF16)
            for d in far_first:
                copy(p1.at[p, h, pl.ds(pl.multiple_of(pos[av][d] * slab, slab), slab)],
                     rr.at[p, h, v], rs_s, rs_r.at[p, h], ids[av][d]).start()

        @pl.when(row_here)
        def _():
            own3 = across(a3, p, vs_at, slab)
            for h in range(H):
                far = across(a2, p, pl.multiple_of(theirs + h * part, part), part)
                e = lax.dot_general(pick, far, NT, preferred_element_type=F32)
                own = lax.dot_general(own3, far, NT, preferred_element_type=F32)
                es[p, 0, h] = (2.0 * e).astype(BF16)
                es[p, 1, h] = (own - e).astype(BF16)
            copy(es.at[p], ed.at[p], es_s.at[p], es_r.at[p], sib).start()
            for h in range(H):
                near = across(a2, p, pl.multiple_of(mine + h * part, part), part)
                e = lax.dot_general(pick, near, NT, preferred_element_type=F32)
                cur[h] = 2.0 * e
                rr[p, h, v] = (n1[h, pl.ds(vs_at, slab), :] + d1[p, h, pl.ds(vs_at, slab), :].astype(F32)
                               - e).astype(BF16)

        left(line, ax_s)
        left(line, au_s)
        left(h1.at[p], dd_s.at[p])

        @pl.when(row_here)
        def _():
            left(es.at[p], es_s.at[p])

        @pl.when(jnp.logical_not(row_here))
        def _():
            got(ed.at[p], es_r.at[p])
            for h in range(H):
                cur[h] = ed[p, 0, h].astype(F32)
                rr[p, h, v] = (n1[h, pl.ds(vs_at, slab), :] + ed[p, 1, h].astype(F32)).astype(BF16)

        if last:
            got(vz.at[pl.ds(0, G - 1)], vs_r.at[0])
            vs[c] = jnp.sum(vz[...], axis=0)
            copy(vs.at[c], vs.at[c], sb_s, sb_r, sib).start()
            got(vs.at[0], sb_r)
            vy[y] = (vs[0] + vs[1])[:, :LANES]
            for d in far_first:
                copy(vy.at[y], vy.at[y], vs_s.at[2], vs_r.at[2], ids["y"][d]).start()
            mid = jnp.where(x * slab < half, vs[0], vs[1])
            f = branches[s].astype(F32)
            grown = f * mid[0:1, :] + (1.0 - f) * (2.0 * mid[1:2, :] - mid[0:1, :])
            shown = iota((slab, half), 1) == lax.rem(x * slab, half) + iota((slab, half), 0)
            column = jnp.sum(jnp.where(shown, grown, 0.0), axis=1, keepdims=True)
            eye = iota((slab, slab), 0) == iota((slab, slab), 1)
            occ[...] = jnp.sum(jnp.where(eye, column, 0.0), axis=0, keepdims=True)

        f = branches[s].astype(F32)
        fa, fb = 2.0 * f - 1.0, 2.0 - 2.0 * f
        tall = min(slab, B)
        cb = (u * bs + c * half) // B
        for h in range(H):
            at2, at3 = xs, pl.multiple_of(v * slab, slab)
            got(rr.at[p, h, pl.ds(0, G - 1)], rs_r.at[p, h])
            now = cur[h]
            grown = fa * (jnp.sum(rr[p, h].astype(F32), axis=0) + now) + fb * now
            if last:
                grown = jnp.where(v * bs + x * slab + iota((slab, part), 0)
                                  == u * bs + c * half + h * part + iota((slab, part), 1), 0.0, grown)
            for r in range(0, slab, tall):
                rb = (v * bs + x * slab + r) // B
                for q in range(part // B):
                    cs = slice(q * B, (q + 1) * B)
                    new = (grown[r:r + tall, cs] * keep[s, rb, cb + h * (part // B) + q].astype(F32)).astype(BF16)
                    if last:
                        out[r:r + tall, h * part + q * B:h * part + (q + 1) * B] = new
                    else:
                        a2[n, h, pl.ds(pl.multiple_of(at2 + r, tall), tall), cs] = new
                        a3[n, h, pl.ds(pl.multiple_of(at3 + r, tall), tall), cs] = new
            if s == STEPS - 2 and h == H - 1:
                squares, diagonal = note_traces(n)
                lane, deep = iota((1, half), 1), iota((8, half), 0)
                trow = jnp.zeros((1, half), F32)
                for i in range(STEPS):
                    trow = trow + jnp.where(lane == 2 * i, t_one[i], 0.0) + jnp.where(lane == 2 * i + 1, t_two[i], 0.0)
                vx[x] = (jnp.where(deep == 0, squares, 0.0) + jnp.where(deep == 1, diagonal, 0.0)
                         + jnp.where(deep == 2, trow, 0.0))
                for d in far_first:
                    copy(vx.at[x], vx.at[x], vs_s.at[1], vs_r.at[1], ids["x"][d]).start()
            if not last:
                gather(n, av, h)
        if s < STEPS - 2:
            note_traces(n)

    got(vy.at[pl.ds(0, G - 1)], vs_r.at[2])
    tr = jnp.sum(vy[...], axis=0)[2:3, :] * (1.0 / order)
    lane, deep = iota((STEPS, LANES), 1), iota((STEPS, LANES), 0)
    for k in range(2):
        traces[:, k:k + 1] = jnp.sum(jnp.where(lane == 2 * deep + k, tr, 0.0), axis=1, keepdims=True)
    left(line, rs_s)
    left(vx.at[pl.ds(0, G - 1)], vs_s.at[1])
    left(vz.at[pl.ds(0, G - 1)], vs_s.at[0])
    left(vy.at[pl.ds(0, G - 1)], vs_s.at[2])
    left(vs.at[0], sb_s)


def body(G, density, branches, keep):
    slab, half = density.shape
    bs, part = 2 * half, half // H
    v, dma = pltpu.VMEM, pltpu.SemaphoreType.DMA
    vmem, hbm = pl.BlockSpec(memory_space=pltpu.VMEM), pl.BlockSpec(memory_space=pltpu.HBM)
    purified, traces, occ = pl.pallas_call(
        functools.partial(kernel, G, bs),
        out_shape=(jax.ShapeDtypeStruct((slab, half), BF16),
                   jax.ShapeDtypeStruct((STEPS, 2), F32),
                   jax.ShapeDtypeStruct((1, slab), F32)),
        in_specs=[hbm, hbm, hbm],
        out_specs=(vmem, vmem, vmem),
        scratch_shapes=[
            v((2, H, bs, part), BF16), v((2, H, bs, part), BF16), v((2, H, bs, part), BF16), v((H, bs, part), F32),
            v((2, H, bs, part), BF16), v((2, H, bs, part), BF16), v((H, slab, part), F32),
            v((2, 2, H, slab, part), BF16), v((2, 2, H, slab, part), BF16),
            v((2, H, G, slab, part), BF16),
            v((G, 8, half), F32), v((G, 8, half), F32), v((2, 8, half), F32), v((G, 8, LANES), F32),
            pltpu.SMEM(branches.shape, jnp.int32), pltpu.SMEM(keep.shape, jnp.int32),
            dma((2 * H + 2,)), dma, dma((2,)), dma, dma((2,)), dma, dma((2, H)), dma((2,)), dma((2, H)),
            dma((2,)), dma((2,)), dma((3,)), dma((3,)), dma, dma,
        ],
        compiler_params=pltpu.CompilerParams(
            collective_id=0, has_side_effects=True, vmem_limit_bytes=55168 * 1024),
        name="purify",
    )(density, branches, keep)
    return purified, traces, occ.reshape(slab)


def solution(mesh):
    G = mesh.shape["col"] // 2
    return jax.shard_map(
        functools.partial(body, G),
        mesh=mesh,
        in_specs=(P("row", "col"), P(), P()),
        out_specs=(P("row", "col"), P(), P("row")),
        check_vma=False,
    )
```

time: 95.9 us -> 94.9 us (0.990)
    unnamed x7 -> x5, local copies, waits for them, and re-layouts: 3.2 us -> 2.42 us
where the time goes in v2:
time: 94.9 us; the launch traced here: 94.7 us
  Pallas kernels  91.6 us (97%)
  local copies, waits for them, and re-layouts  2.42 us (3%)
    pallas_call x1, Pallas kernels, body(): pl.pallas_call(functools.partial(kernel, G, bs), out_shape=(jax.ShapeDtyp...  91.6 us
    unnamed x5, local copies, waits for them, and re-layouts  2.42 us

profile of v2, /device:TPU:1, one launch (start us, length us, event | category | flops | bytes accessed | tf_op | source)
XLA Modules:
  0.0 94.7 jit_solution(18101176665134420563)
XLA Ops:
  0.6 0.0 copy-start
  0.6 0.6 copy-done
  1.3 91.6 %purify.1 = (bf16[64,256]{1,0:T(8,128)(2,1)S(1)}, f32[4,2]{1,0:T(4,128)S(1)}, f32[1,64]{1,0:T(1,128)S(1)}) custom-call(bf16[64,256]{1,0:T(8,128)(2,1)} %dens.1, s32[4]{0:T(128)S(1)} %copy-done, s32[4,32,32]{2,1,0:T(8,128)} %keep_in.1), custom_call_target="tpu_custom_call" | custom-call | tf_op jit(solution)/shard_map/purify/pallas_call | solution.py:244
  92.9 0.6 copy.6
  93.5 0.6 copy.9
  94.1 0.5 copy.10
Async XLA Ops:
  0.6 0.7 copy-start

commit v3 on v2

--- a/solution.py
+++ b/solution.py
@@ -32,9 +32,10 @@
         return {"row": ay * G + ax, "col": az * 2 + ac}
 
     far_first = sorted(range(1, G), key=lambda d: -min(d, G - d))
-    pos = {"x": {d: lax.rem(x + d, G) for d in far_first},
-           "y": {d: lax.rem(y + d, G) for d in far_first},
-           "z": {d: lax.rem(z + d, G) for d in far_first}}
+    way = {d: d + c * (G - 2 * d) for d in far_first}
+    pos = {"x": {d: lax.rem(x + way[d], G) for d in far_first},
+           "y": {d: lax.rem(y + way[d], G) for d in far_first},
+           "z": {d: lax.rem(z + way[d], G) for d in far_first}}
     ids = {"x": {d: dev(pos["x"][d], y, z, c) for d in far_first},
            "y": {d: dev(x, pos["y"][d], z, c) for d in far_first},
            "z": {d: dev(x, y, pos["z"][d], c) for d in far_first}}

time: 94.9 us -> 94.6 us (level)
  no operation moved by 1% of the time
where the time goes in v3:
time: 94.6 us; the launch traced here: 94.4 us
  Pallas kernels  91.3 us (97%)
  local copies, waits for them, and re-layouts  2.42 us (3%)
    pallas_call x1, Pallas kernels, body(): pl.pallas_call(functools.partial(kernel, G, bs), out_shape=(jax.ShapeDtyp...  91.3 us
    unnamed x5, local copies, waits for them, and re-layouts  2.42 us

profile of v3, /device:TPU:1, one launch (start us, length us, event | category | flops | bytes accessed | tf_op | source)
XLA Modules:
  0.0 94.4 jit_solution(5967304041389932146)
XLA Ops:
  0.6 0.0 copy-start
  0.6 0.6 copy-done
  1.3 91.3 %purify.1 = (bf16[64,256]{1,0:T(8,128)(2,1)S(1)}, f32[4,2]{1,0:T(4,128)S(1)}, f32[1,64]{1,0:T(1,128)S(1)}) custom-call(bf16[64,256]{1,0:T(8,128)(2,1)} %dens.1, s32[4]{0:T(128)S(1)} %copy-done, s32[4,32,32]{2,1,0:T(8,128)} %keep_in.1), custom_call_target="tpu_custom_call" | custom-call | tf_op jit(solution)/shard_map/purify/pallas_call | solution.py:245
  92.6 0.6 copy.6
  93.3 0.6 copy.9
  93.9 0.5 copy.10
Async XLA Ops:
  0.6 0.7 copy-start
